TPU v7x, 32 devices: a whole 2x2x4 slice. The times are simulated.
32 devices in a mesh: frame: 16 (over z, x, core), head: 2 (over y).
Axes of the slice: x: 2, y: 2, z: 4, core: 2. Of those that a mesh axis runs over, the one named last changes fastest.
Arguments:
- queries: bfloat16 [16384, 256], P(('frame', 'head')), may hold values from -8 to 8
- key_vectors: bfloat16 [16384, 256], P(('frame', 'head')), may hold values from -5 to 5
- value_vectors: bfloat16 [16384, 256], P(('frame', 'head')), may hold values from -6 to 6
- tile_lists: int32 [2, 128, 20], P('head', 'frame'), may hold values from 0 to 127, as said below
- live_slots: int32 [2, 128], P('head', 'frame'), may hold values from 2 to 20
Outputs:
- attended: bfloat16 [16384, 256], P(('frame', 'head'))
Inputs may be any that keep to these rules, and one draw needn't show every extreme that they name: `tile_lists`: slot 0 of query tile t holds t; the slots below live_slots hold distinct tiles u with |u - t| <= 32; the other slots hold t.
All inputs are finite; a program needn't handle non-finite values.
Results may differ from a plain program's by a relative error of at most 0.0045.
Values may be sent and summed in bfloat16 or wider, within the bound.
No kernel may reach another device: no remote copies, remote signals or barrier semaphores. Data moves between devices by JAX's collectives and lax.ppermute only.
A program may use at most 64 MiB of HBM per device.

v0:
```python
import functools
import math

import jax
import jax.numpy as jnp
import numpy as np
from jax import lax
from jax.experimental import pallas as pl
from jax.experimental.pallas import tpu as pltpu
from jax.sharding import PartitionSpec as P

TILE = 128
HEAD_DIM = 128
REACH = 32
PLANE = 4
GROUP = 4
LISTS = 4
FAR_OFF = 1e30
FACTOR = math.log2(math.e) / math.sqrt(HEAD_DIM)
VMEM = pl.BlockSpec(memory_space=pltpu.VMEM)
SMEM = pl.BlockSpec(memory_space=pltpu.SMEM)


def shard_table():
    table = np.zeros((PLANE, 2 * PLANE + 1), np.int32)
    for place in range(PLANE):
        x, core = divmod(place, 2)
        for distance in range(-PLANE, PLANE + 1):
            plane, there = divmod(place + distance, PLANE)
            same_x, same_core = there // 2 == x, there % 2 == core
            phase = 0
            if plane == 0:
                spot = int(same_core) if same_x else (4 if same_core else 5)
            elif not same_x:
                phase, spot = 1, 0 if same_core else 1
            elif (plane < 0) == (core == 0):
                spot = 2 + int(same_core)
            else:
                spot = 6
            table[place, distance + PLANE] = phase + 4 * spot
    return table.reshape(-1)


def params(mib):
    return pltpu.CompilerParams(vmem_limit_bytes=mib * 2**20)


def cost():
    return pl.CostEstimate(flops=0, bytes_accessed=0, transcendentals=0)


def tile_kernel(heads, flip, *refs):
    out_ref = refs[-1]
    tiles = refs[0].shape[0] // TILE
    for head in range(heads):
        for which, flipped in enumerate(flip):
            for tile in range(tiles):
                block = refs[which][
                    tile * TILE : (tile + 1) * TILE, head * HEAD_DIM : (head + 1) * HEAD_DIM
                ]
                at = (tile * heads + head) * len(flip) + which
                out_ref[at] = block.T if flipped else block


def as_tiles(arrays, flip):
    rows, width = arrays[0].shape
    heads = width // HEAD_DIM
    count = len(arrays) * heads * rows // TILE
    return pl.pallas_call(
        functools.partial(tile_kernel, heads, flip),
        in_specs=[VMEM] * len(arrays),
        out_specs=VMEM,
        out_shape=jax.ShapeDtypeStruct((count, TILE, HEAD_DIM), arrays[0].dtype),
        compiler_params=params(4),
    )(*arrays)


def list_kernel(heads, length, where_ref, lists_ref, live_ref, table_ref, ends, metas, places):
    tiles = live_ref.shape[0]
    part_tiles = tiles // heads
    frame, head = where_ref[0], where_ref[1]
    base = lax.rem(frame, PLANE) * (2 * PLANE + 1) + PLANE - frame
    targets = range(LISTS * heads)
    for target in targets:
        ends[target] = target * length
    for row in range(tiles):
        part, inner = divmod(row, part_tiles)

        def slot_step(slot, carry, row=row, part=part, inner=inner):
            listed = lists_ref[row, slot]
            within = listed & (tiles - 1)
            rank = within >> int(math.log2(part_tiles))
            spot = ((within & (part_tiles - 1)) * heads + head) * 2
            entry = table_ref[base + (listed >> int(math.log2(tiles)))]
            step = (rank - head) & (heads - 1)
            turn = (rank - part) & (heads - 1)
            own = turn == 0
            query = (turn * part_tiles + inner) * heads + head
            query = jnp.where(own, query, query - heads * part_tiles)
            target = step * LISTS + 2 * (entry & 3) + jnp.where(own, 1, 0)
            at = ends[target]
            places[at] = (entry >> 2) * (2 * tiles) + spot
            metas[at >> 2] = query * 8 + (at & (GROUP - 1))
            ends[target] = at + 1
            return carry

        lax.fori_loop(0, live_ref[row], slot_step, 0)
        for target in targets:
            at = ends[target]
            up = (at + GROUP - 1) & -GROUP
            filler = places[jnp.maximum(at - 1, 0)]
            for other in range(GROUP - 1):
                spare = LISTS * heads * length
                places[jnp.where(at + other < up, at + other, spare)] = filler
            ends[target] = up
    for target in targets:
        ends[target] = (ends[target] - target * length) >> 2


def work_lists(frame, head, tile_lists, live_slots, heads):
    tiles, slots = tile_lists.shape
    assert tiles & (tiles - 1) == 0 and heads & (heads - 1) == 0 and GROUP == 4
    length = tiles * (slots // GROUP + 1) * GROUP
    total = LISTS * heads * length
    ends, metas, places = pl.pallas_call(
        functools.partial(list_kernel, heads, length),
        in_specs=[SMEM] * 4,
        out_specs=[SMEM] * 3,
        out_shape=[
            jax.ShapeDtypeStruct((LISTS * heads,), jnp.int32),
            jax.ShapeDtypeStruct((total // GROUP,), jnp.int32),
            jax.ShapeDtypeStruct((total + 1,), jnp.int32),
        ],
        compiler_params=params(4),
        cost_estimate=cost(),
    )(jnp.stack((frame, head)), tile_lists, live_slots, jnp.asarray(shard_table()))
    arrays = ends, metas, places[:total]
    return jnp.concatenate([array.reshape(heads, -1) for array in arrays], axis=1)


def packed(numbers):
    rows = -(-numbers.shape[0] // TILE)
    numbers = jnp.pad(numbers, (0, rows * TILE - numbers.shape[0])).reshape(rows, TILE)
    digits = jnp.concatenate((numbers & 255, numbers >> 8)).astype(jnp.bfloat16)
    return jnp.pad(digits, ((0, -2 * rows % 16), (0, 0)))


def unpacked(block, count):
    rows = -(-count // TILE)
    digits = block.astype(jnp.int32)
    return (digits[:rows] + digits[rows : 2 * rows] * 256).reshape(-1)[:count]


def phase_kernel(which, pieces, begins, ends, lists, q_ref, *refs):
    refs = list(refs)
    state = [refs.pop(0) for _ in range(0 if begins else 3)]
    parts = [refs.pop(0) for _ in range(pieces)]
    out_ref, stats_ref = [refs.pop(0) for _ in range(2)] if ends else [None] * 2
    top_ref, total_ref, sum_ref, scores, high, weights, shrinks = refs[:7]
    window = refs[7] if pieces > 1 else parts[0]
    tiles = q_ref.shape[0]
    heads, width = lists.shape
    length = (width - LISTS) // (LISTS * (GROUP + 1))

    at = 0
    for part in parts if pieces > 1 else ():
        window[at : at + part.shape[0]] = part[...]
        at += part.shape[0]
    if begins:
        top_ref[...] = jnp.full(top_ref.shape, -FAR_OFF, jnp.float32)
        total_ref[...] = jnp.zeros(total_ref.shape, jnp.float32)
        sum_ref[...] = jnp.zeros(sum_ref.shape, jnp.float32)
    else:
        for ref, old in zip((top_ref, total_ref, sum_ref), state):
            ref[...] = old[...]

    starts = [jnp.int32(0)]
    for head in range(heads):
        starts.append(starts[-1] + lists[head, which])

    def item_of(item):
        row, index = jnp.int32(0), item
        for head in range(1, heads):
            row = jnp.where(item >= starts[head], head, row)
            index = jnp.where(item >= starts[head], item - starts[head], index)
        real = item < starts[heads]
        row, index = jnp.where(real, row, 0), jnp.where(real, index, 0)
        meta = lists[row, LISTS + which * length + index]
        at = LISTS * (1 + length) + (which * length + index) * GROUP
        tile = jnp.where(real, meta >> 3, 0)
        spots = [jnp.where(real, lists[row, at + slot], 0) for slot in range(GROUP)]
        return tile, jnp.where(real, meta & 7, -1), spots

    def score(entry):
        tile, _, spots = entry
        keys = jnp.concatenate([window[spot] for spot in spots])
        block = jnp.dot(keys, q_ref[tile], preferred_element_type=jnp.float32)
        top = jnp.max(block.reshape(-1, 8, TILE), axis=0)
        return block, jnp.max(top, axis=0, keepdims=True)

    def weigh(entry, block, peak):
        tile, last, _ = entry
        old = top_ref[tile]
        top = jnp.maximum(old, jnp.where(last < 0, -FAR_OFF, peak))
        shrink = jnp.exp2((old - top) * FACTOR)
        total = total_ref[tile] * shrink
        parts = []
        for slot in range(GROUP):
            shift = jnp.where(slot <= last, top, FAR_OFF)
            weight = jnp.exp2((block[slot * TILE : (slot + 1) * TILE] - shift) * FACTOR)
            total = total + jnp.sum(weight.reshape(-1, 8, TILE), axis=0)
            parts.append(weight.astype(jnp.bfloat16))
        top_ref[tile] = top
        total_ref[tile] = total
        return jnp.concatenate(parts), shrink

    def collect(entry, weight, shrink):
        tile, _, spots = entry
        values = jnp.concatenate([window[spot + 1] for spot in spots], axis=1)
        product = jnp.dot(values, weight, preferred_element_type=jnp.float32)
        sum_ref[tile] = sum_ref[tile] * shrink + product

    def store_scores(pair):
        for number, (block, peak) in enumerate(pair):
            scores[number], high[number] = block, peak

    def store_weights(pair):
        for number, (weight, shrink) in enumerate(pair):
            weights[number], shrinks[number] = weight, shrink

    ahead = [item_of(0), item_of(1)]
    second = [item_of(2), item_of(3)]
    first = [score(entry) for entry in ahead]
    store_scores([score(entry) for entry in second])
    store_weights([weigh(entry, *made) for entry, made in zip(ahead, first)])

    def step(pair, entries):
        collected, weighed = entries[:2], entries[2:]
        scored = [item_of(2 * pair + 4), item_of(2 * pair + 5)]
        made = [(scores[number], high[number]) for number in range(2)]
        formed = [(weights[number], shrinks[number]) for number in range(2)]
        blocks = [score(entry) for entry in scored]
        following = [weigh(entry, *item) for entry, item in zip(weighed, made)]
        for entry, item in zip(collected, formed):
            collect(entry, *item)
        store_scores(blocks)
        store_weights(following)
        return tuple(weighed) + tuple(scored)

    lax.fori_loop(0, (starts[heads] + 1) >> 1, step, tuple(ahead + second))
    if ends:
        for tile in range(tiles):
            total = jnp.sum(total_ref[tile], axis=0, keepdims=True)
            share = jnp.where(total > 0, 1.0 / jnp.where(total > 0, total, 1.0), 0.0)
            out_ref[tile] = (sum_ref[tile] * share).astype(out_ref.dtype)
            stats_ref[tile, 0:1] = total
            stats_ref[tile, 1:2] = top_ref[tile]


def attend(lists, which, queries, state, pieces, ends):
    tiles = queries.shape[0]
    begins = state is None
    held = [
        jax.ShapeDtypeStruct((tiles, 1, TILE), jnp.float32),
        jax.ShapeDtypeStruct((tiles, 8, TILE), jnp.float32),
        jax.ShapeDtypeStruct((tiles, HEAD_DIM, TILE), jnp.float32),
    ]
    scratch = [
        pltpu.VMEM((2, GROUP * TILE, TILE), jnp.float32),
        pltpu.VMEM((2, 1, TILE), jnp.float32),
        pltpu.VMEM((2, GROUP * TILE, TILE), queries.dtype),
        pltpu.VMEM((2, 1, TILE), jnp.float32),
    ]
    if len(pieces) > 1:
        rows = sum(piece.shape[0] for piece in pieces)
        scratch.append(pltpu.VMEM((rows, TILE, TILE), queries.dtype))
    if ends:
        scratch = [pltpu.VMEM(array.shape, array.dtype) for array in held] + scratch
        held = [
            jax.ShapeDtypeStruct((tiles, HEAD_DIM, TILE), queries.dtype),
            jax.ShapeDtypeStruct((tiles, 2, TILE), jnp.float32),
        ]
    return pl.pallas_call(
        functools.partial(phase_kernel, which, len(pieces), begins, ends),
        in_specs=[SMEM] + [VMEM] * (1 + len(pieces) + (0 if begins else 3)),
        out_specs=[VMEM] * len(held),
        out_shape=held,
        scratch_shapes=scratch,
        compiler_params=params(10),
        cost_estimate=cost(),
    )(lists, queries, *([] if begins else state), *pieces)


def merge_kernel(count, *refs):
    out_ref = refs[-1]
    values, stats = [refs[first : 2 * count : 2] for first in range(2)]
    tiles = values[0].shape[0]
    heads = out_ref.shape[1] // HEAD_DIM
    for tile in range(tiles):
        top = stats[0][tile, 1:2]
        for ref in stats[1:]:
            top = jnp.maximum(top, ref[tile, 1:2])
        shares = [ref[tile, 0:1] * jnp.exp2((ref[tile, 1:2] - top) * FACTOR) for ref in stats]
        whole = sum(shares[1:], shares[0])
        out = jnp.zeros((HEAD_DIM, TILE), jnp.float32)
        for value, share in zip(values, shares):
            out = out + value[tile].astype(jnp.float32) * (share / whole)
        inner, head = divmod(tile, heads)
        out_ref[
            inner * TILE : (inner + 1) * TILE, head * HEAD_DIM : (head + 1) * HEAD_DIM
        ] = out.T.astype(out_ref.dtype)


def merge(parts, rows, heads):
    flat = [array for part in parts for array in part]
    return pl.pallas_call(
        functools.partial(merge_kernel, len(parts)),
        in_specs=[VMEM] * len(flat),
        out_specs=VMEM,
        out_shape=jax.ShapeDtypeStruct((rows, heads * HEAD_DIM), flat[0].dtype),
        compiler_params=params(6),
    )(*flat)


def moved(block, axis, source):
    size = lax.axis_size(axis)
    route = [(source(i), i) for i in range(size) if 0 <= source(i) < size]
    return lax.ppermute(block, axis, route)


def body(queries, key_vectors, value_vectors, tile_lists, live_slots):
    heads = lax.axis_size("head")
    frame = lax.axis_index("frame")
    head = lax.axis_index("head")
    shard_tiles = tile_lists.shape[1]
    assert shard_tiles * PLANE == REACH and lax.axis_size("frame") % PLANE == 0

    def from_head(block, step):
        return moved(block, "head", lambda i: (i - step) % heads)

    def core_swap(block):
        return moved(block, "frame", lambda i: i ^ 1)

    own = as_tiles((key_vectors, value_vectors), (False, True))
    size = own.shape[0]
    cut = size // 2
    across = moved(own, "frame", lambda i: i ^ 2)
    chip = jnp.concatenate((core_swap(own), own))
    level = moved(chip, "frame", lambda i: i - PLANE if i % 2 == 0 else i + PLANE)

    listed, live, _ = lax.optimization_barrier((tile_lists[0], live_slots[0], chip))
    lists = work_lists(frame, head, listed, live, heads)
    q_own = as_tiles((queries,), (True,))
    blocks = [
        from_head(jnp.concatenate((q_own.reshape(-1, TILE), packed(lists[step]))), step)
        for step in range(1, heads)
    ]
    blocks, _ = lax.optimization_barrier((blocks, level))
    q_parts, by_head = [], [lists[:1]]
    for block in blocks:
        q_rows = shard_tiles * TILE
        q_parts.append(block[:q_rows].reshape(q_own.shape))
        by_head.append(unpacked(block[q_rows:], lists.shape[1])[None])
    q_rest, by_head = jnp.concatenate(q_parts), jnp.concatenate(by_head)

    far_z = moved(across[:cut], "frame", lambda i: i - PLANE if i % PLANE < 2 else i + PLANE)
    straight = moved(own[cut:], "frame", lambda i: i - 2 if i % PLANE < 2 else i + 2)
    near = [chip, level, across, core_swap(across), core_swap(level[:size])]
    state = attend(by_head, 0, q_rest, None, near, False)
    far_z, straight, state = lax.optimization_barrier((far_z, straight, state))
    far = jnp.concatenate((far_z, straight))
    far = [far, core_swap(far)]
    rest = attend(by_head, 2, q_rest, state, far, True)
    parts = [None]
    for step in range(1, heads):
        cut = slice((step - 1) * shard_tiles, step * shard_tiles)
        parts.append([from_head(array[cut], -step) for array in rest])
    q_own, _ = lax.optimization_barrier((q_own, rest))
    state = attend(by_head, 1, q_own, None, near, False)
    parts[0] = attend(by_head, 3, q_own, state, far, True)
    return merge(parts, queries.shape[0], heads)


def solution(mesh):
    placed = (
        P(("frame", "head"), None),
        P(("frame", "head"), None),
        P(("frame", "head"), None),
        P("head", "frame", None),
        P("head", "frame"),
    )
    return jax.shard_map(
        body, mesh=mesh, in_specs=placed, out_specs=P(("frame", "head"), None), check_vma=False
    )
```

profile of v0, /device:TPU:18, one launch (start us, length us, event | category | flops | bytes accessed | tf_op | source)
XLA Modules:
  0.0 43.4 jit_solution(6368381980167753768)
XLA Ops:
  0.0 1.0 %copy-done.1 = bf16[512,256]{1,0:T(8,128)(2,1)S(1)} copy-done((bf16[512,256]{1,0:T(8,128)(2,1)S(1)}, bf16[512,256]{1,0:T(8,128)(2,1)}, u32[]{:S(2)}) %copy-start.1) | copy-done | bytes 262168
  1.0 0.9 %copy-done.2 = bf16[512,256]{1,0:T(8,128)(2,1)S(1)} copy-done((bf16[512,256]{1,0:T(8,128)(2,1)S(1)}, bf16[512,256]{1,0:T(8,128)(2,1)}, u32[]{:S(2)}) %copy-start.2) | copy-done | bytes 262168
  1.9 0.1 shard_map.64
  2.1 0.1 collective-permute-start
  2.2 0.6 %collective-permute-start.3 = (bf16[16,128,128]{2,1,0:T(8,128)(2,1)S(1)}, bf16[16,128,128]{2,1,0:T(8,128)(2,1)S(1)}, u32[]{:S(2)}, u32[]{:S(2)}) collective-permute-start(bf16[16,128,128]{2,1,0:T(8,128)(2,1)S(1)} %shard_map.64), channel_id=1, source_target_pairs={{4,0},{6,2},{0,4},{2,6},{12,8},{14,10},{8,12},{10,14},{20,16},{22,... | collective-permute-start | bytes 1572872 | tf_op jit(solution)/shard_map/ppermute | solution.py:328
  2.8 0.1 shard_map.66.q_ref
  2.9 1.2 %collective-permute-done = bf16[16,128,128]{2,1,0:T(8,128)(2,1)S(1)} collective-permute-done((bf16[16,128,128]{2,1,0:T(8,128)(2,1)S(1)}, bf16[16,128,128]{2,1,0:T(8,128)(2,1)S(1)}, u32[]{:S(2)}, u32[]{:S(2)}) %collective-permute-start) | collective-permute-done | bytes 524320 | tf_op jit(solution)/shard_map/ppermute | solution.py:328
  4.0 0.1 pad_maximum_fusion.refs_0_
  4.1 3.5 %collective-permute-start.2 = (bf16[32,128,128]{2,1,0:T(8,128)(2,1)S(1)}, bf16[32,128,128]{2,1,0:T(8,128)(2,1)S(1)}, u32[]{:S(2)}, u32[]{:S(2)}) collective-permute-start(bf16[32,128,128]{2,1,0:T(8,128)(2,1)S(1)} %pad_maximum_fusion.refs_0_), channel_id=1, source_target_pairs={{10,2},{14,6},{0,8},{18,10},{4,12},{22,14},{8,16},{26,18},{12,20},... | collective-permute-start | bytes 3145736 | tf_op jit(solution)/shard_map/ppermute | solution.py:328
  7.7 0.1 pad_add_fusion.2.where_ref
  7.7 0.6 %copy-done.3 = s32[1,8,20]{2,1,0:T(8,128)S(1)} copy-done((s32[1,8,20]{2,1,0:T(8,128)S(1)}, s32[1,8,20]{2,1,0:T(8,128)}, u32[]{:S(2)}) %copy-start.3) | copy-done | bytes 664
  8.3 0.1 copy-done.4
  8.4 4.2 %shard_map.65 = (s32[8]{0:T(128)S(1)}, s32[384]{0:T(512)S(1)}, s32[1537]{0:T(1024)S(1)}) custom-call(s32[2]{0:T(128)S(1)} %pad_add_fusion.2.where_ref, s32[8,20]{1,0:T(8,128)S(1)} %bitcast.20, s32[8]{0:T(128)S(1)} %bitcast.21, s32[36]{0:T(128)S(1)} %copy-done.5), custom_call_target="tpu_custom_call" | custom-call | tf_op jit(solution)/shard_map/pallas_call | solution.py:125
  12.6 0.1 reshape.25
  12.7 0.1 reshape.26
  12.8 0.1 pad_add_fusion
  12.9 1.7 %collective-permute-start.1 = (bf16[1040,128]{1,0:T(8,128)(2,1)S(1)}, bf16[1040,128]{1,0:T(8,128)(2,1)S(1)}, u32[]{:S(2)}, u32[]{:S(2)}) collective-permute-start(bf16[1040,128]{1,0:T(8,128)(2,1)S(1)} %pad_maximum_fusion.1), channel_id=1, source_target_pairs={{1,0},{0,1},{3,2},{2,3},{5,4},{4,5},{7,6},{6,7},{9,8},{8,9},{11,10... | collective-permute-start | bytes 798728 | tf_op jit(solution)/shard_map/ppermute | solution.py:328
  14.6 1.9 %collective-permute-start.5 = (bf16[8,128,128]{2,1,0:T(8,128)(2,1)S(1)}, bf16[8,128,128]{2,1,0:T(8,128)(2,1)S(1)}, u32[]{:S(2)}, u32[]{:S(2)}) collective-permute-start(bf16[8,128,128]{2,1,0:T(8,128)(2,1)S(1)} %slice.49), channel_id=1, source_target_pairs={{8,4},{10,6},{4,8},{6,10},{16,12},{18,14},{12,16},{14,18},{24,20},... | collective-permute-start | bytes 786440 | tf_op jit(solution)/shard_map/ppermute | solution.py:328
  16.6 3.9 %collective-permute-start.4 = (bf16[8,128,128]{2,1,0:T(8,128)(2,1)S(1)}, bf16[8,128,128]{2,1,0:T(8,128)(2,1)S(1)}, u32[]{:S(2)}, u32[]{:S(2)}) collective-permute-start(bf16[8,128,128]{2,1,0:T(8,128)(2,1)S(1)} %slice.48), channel_id=1, source_target_pairs={{12,4},{14,6},{0,8},{2,10},{20,12},{22,14},{8,16},{10,18},{28,20},... | collective-permute-start | bytes 786440 | tf_op jit(solution)/shard_map/ppermute | solution.py:328
  20.5 0.1 collective-permute-start.6
  20.6 3.1 %collective-permute-done.2.refs_1_ = bf16[32,128,128]{2,1,0:T(8,128)(2,1)S(1)} collective-permute-done((bf16[32,128,128]{2,1,0:T(8,128)(2,1)S(1)}, bf16[32,128,128]{2,1,0:T(8,128)(2,1)S(1)}, u32[]{:S(2)}, u32[]{:S(2)}) %collective-permute-start.2) | collective-permute-done | bytes 1048608 | tf_op jit(solution)/shard_map/ppermute | solution.py:328
  23.7 0.1 collective-permute-start.7
  23.8 1.8 %collective-permute-done.7.refs_4_ = bf16[16,128,128]{2,1,0:T(8,128)(2,1)S(1)} collective-permute-done((bf16[16,128,128]{2,1,0:T(8,128)(2,1)S(1)}, bf16[16,128,128]{2,1,0:T(8,128)(2,1)S(1)}, u32[]{:S(2)}, u32[]{:S(2)}) %collective-permute-start.7) | collective-permute-done | bytes 524320 | tf_op jit(solution)/shard_map/ppermute | solution.py:328
  25.7 3.7 %shard_map.67 = (f32[8,1,128]{2,1,0:T(1,128)S(1)}, f32[8,8,128]{2,1,0:T(8,128)S(1)}, f32[8,128,128]{2,1,0:T(8,128)S(1)}) custom-call(s32[2,964]{1,0:T(2,128)S(1)} %pad_add_fusion.1.lists, bf16[8,128,128]{2,1,0:T(8,128)(2,1)S(1)} %bitcast.17, bf16[32,128,128]{2,1,0:T(8,128)(2,1)S(1)} %pad_maximum_fusion.refs_0_, ...), custom_call_target="tpu_custom_call" | custom-call | tf_op jit(solution)/shard_map/pallas_call | solution.py:283
  29.5 0.1 collective-permute-start.8
  29.6 1.9 %collective-permute-done.8.refs_4_ = bf16[16,128,128]{2,1,0:T(8,128)(2,1)S(1)} collective-permute-done((bf16[16,128,128]{2,1,0:T(8,128)(2,1)S(1)}, bf16[16,128,128]{2,1,0:T(8,128)(2,1)S(1)}, u32[]{:S(2)}, u32[]{:S(2)}) %collective-permute-start.8) | collective-permute-done | bytes 524320 | tf_op jit(solution)/shard_map/ppermute | solution.py:328
  31.5 2.4 %shard_map.68 = (bf16[8,128,128]{2,1,0:T(8,128)(2,1)S(1)}, f32[8,2,128]{2,1,0:T(2,128)S(1)}) custom-call(s32[2,964]{1,0:T(2,128)S(1)} %pad_add_fusion.1.lists, bf16[8,128,128]{2,1,0:T(8,128)(2,1)S(1)} %bitcast.18, f32[8,1,128]{2,1,0:T(1,128)S(1)} %get-tuple-element.36.refs_0_, f32[8,8,128]{2,1,0:T(8,128)S(1)} %get-tuple-element.37.refs_1_, ...), custom_call_target="tpu_custom_call" | custom-call | tf_op jit(solution)/shard_map/pallas_call | solution.py:283
  33.9 1.3 %collective-permute-start.9 = (bf16[8,128,128]{2,1,0:T(8,128)(2,1)S(1)}, bf16[8,128,128]{2,1,0:T(8,128)(2,1)S(1)}, u32[]{:S(2)}, u32[]{:S(2)}) collective-permute-start(bf16[8,128,128]{2,1,0:T(8,128)(2,1)S(1)} %get-tuple-element.41), channel_id=1, source_target_pairs={{1,0},{0,1},{3,2},{2,3},{5,4},{4,5},{7,6},{6,7},{9,8},{8,9},{11,10... | collective-permute-start | bytes 786440 | tf_op jit(solution)/shard_map/ppermute | solution.py:328
  35.2 0.8 %collective-permute-start.10 = (f32[8,2,128]{2,1,0:T(2,128)S(1)}, f32[8,2,128]{2,1,0:T(2,128)S(1)}, u32[]{:S(2)}, u32[]{:S(2)}) collective-permute-start(f32[8,2,128]{2,1,0:T(2,128)S(1)} %get-tuple-element.42), channel_id=1, source_target_pairs={{1,0},{0,1},{3,2},{2,3},{5,4},{4,5},{7,6},{6,7},{9,8},{8,9},{11,10... | collective-permute-start | bytes 24584 | tf_op jit(solution)/shard_map/ppermute | solution.py:328
  36.0 4.0 %shard_map.69 = (f32[8,1,128]{2,1,0:T(1,128)S(1)}, f32[8,8,128]{2,1,0:T(8,128)S(1)}, f32[8,128,128]{2,1,0:T(8,128)S(1)}) custom-call(s32[2,964]{1,0:T(2,128)S(1)} %pad_add_fusion.1.lists, bf16[8,128,128]{2,1,0:T(8,128)(2,1)S(1)} %shard_map.66.q_ref, bf16[32,128,128]{2,1,0:T(8,128)(2,1)S(1)} %pad_maximum_fusion.refs_0_, ...), custom_call_target="tpu_custom_call" | custom-call | tf_op jit(solution)/shard_map/pallas_call | solution.py:283
  40.1 2.4 %shard_map.70 = (bf16[8,128,128]{2,1,0:T(8,128)(2,1)S(1)}, f32[8,2,128]{2,1,0:T(2,128)S(1)}) custom-call(s32[2,964]{1,0:T(2,128)S(1)} %pad_add_fusion.1.lists, bf16[8,128,128]{2,1,0:T(8,128)(2,1)S(1)} %shard_map.66.q_ref, f32[8,1,128]{2,1,0:T(1,128)S(1)} %get-tuple-element.44.refs_0_, f32[8,8,128]{2,1,0:T(8,128)S(1)} %get-tuple-element.45.refs_1_, ...), custom_call_target="tpu_custom_call" | custom-call | tf_op jit(solution)/shard_map/pallas_call | solution.py:283
  42.5 0.9 %shard_map.71 = bf16[512,256]{1,0:T(8,128)(2,1)} custom-call(bf16[8,128,128]{2,1,0:T(8,128)(2,1)S(1)} %get-tuple-element.47.refs_0_, f32[8,2,128]{2,1,0:T(2,128)S(1)} %get-tuple-element.48.refs_1_, bf16[8,128,128]{2,1,0:T(8,128)(2,1)S(1)} %collective-permute-done.9.refs_2_, f32[8,2,128]{2,1,0:T(2,128)S(1)} %collective-permute-done.10.refs_3_), custom_call_target="tpu_custom_call" | custom-call | tf_op jit(solution)/shard_map/pallas_call | solution.py:316
  (28 shorter events, 0.3 us)
Async XLA Ops:
  0.0 2.8 %copy-start = (bf16[512,256]{1,0:T(8,128)(2,1)S(1)}, bf16[512,256]{1,0:T(8,128)(2,1)}, u32[]{:S(2)}) copy-start(bf16[512,256]{1,0:T(8,128)(2,1)} %refs_0_.3) | copy-start | bytes 786436
  0.0 1.0 %copy-start.1 = (bf16[512,256]{1,0:T(8,128)(2,1)S(1)}, bf16[512,256]{1,0:T(8,128)(2,1)}, u32[]{:S(2)}) copy-start(bf16[512,256]{1,0:T(8,128)(2,1)} %refs_0_.2) | copy-start | bytes 786436
  1.0 0.9 %copy-start.2 = (bf16[512,256]{1,0:T(8,128)(2,1)S(1)}, bf16[512,256]{1,0:T(8,128)(2,1)}, u32[]{:S(2)}) copy-start(bf16[512,256]{1,0:T(8,128)(2,1)} %refs_1_.1) | copy-start | bytes 786436
  2.1 2.0 %collective-permute-start = (bf16[16,128,128]{2,1,0:T(8,128)(2,1)S(1)}, bf16[16,128,128]{2,1,0:T(8,128)(2,1)S(1)}, u32[]{:S(2)}, u32[]{:S(2)}) collective-permute-start(bf16[16,128,128]{2,1,0:T(8,128)(2,1)S(1)} %shard_map.64), channel_id=1, source_target_pairs={{2,0},{0,2},{6,4},{4,6},{10,8},{8,10},{14,12},{12,14},{18,16},{16,... | collective-permute-start | bytes 1572872 | tf_op jit(solution)/shard_map/ppermute | solution.py:328
  2.2 14.4 %collective-permute-start.3 = (bf16[16,128,128]{2,1,0:T(8,128)(2,1)S(1)}, bf16[16,128,128]{2,1,0:T(8,128)(2,1)S(1)}, u32[]{:S(2)}, u32[]{:S(2)}) collective-permute-start(bf16[16,128,128]{2,1,0:T(8,128)(2,1)S(1)} %shard_map.64), channel_id=1, source_target_pairs={{4,0},{6,2},{0,4},{2,6},{12,8},{14,10},{8,12},{10,14},{20,16},{22,... | collective-permute-start | bytes 1572872 | tf_op jit(solution)/shard_map/ppermute | solution.py:328
  4.1 19.5 %collective-permute-start.2 = (bf16[32,128,128]{2,1,0:T(8,128)(2,1)S(1)}, bf16[32,128,128]{2,1,0:T(8,128)(2,1)S(1)}, u32[]{:S(2)}, u32[]{:S(2)}) collective-permute-start(bf16[32,128,128]{2,1,0:T(8,128)(2,1)S(1)} %pad_maximum_fusion.refs_0_), channel_id=1, source_target_pairs={{10,2},{14,6},{0,8},{18,10},{4,12},{22,14},{8,16},{26,18},{12,20},... | collective-permute-start | bytes 3145736 | tf_op jit(solution)/shard_map/ppermute | solution.py:328
  7.6 0.7 %copy-start.3 = (s32[1,8,20]{2,1,0:T(8,128)S(1)}, s32[1,8,20]{2,1,0:T(8,128)}, u32[]{:S(2)}) copy-start(s32[1,8,20]{2,1,0:T(8,128)} %param.9) | copy-start | bytes 1924
  7.7 0.7 %copy-start.4 = (s32[1,8]{1,0:T(1,128)S(1)}, s32[1,8]{1,0:T(1,128)}, u32[]{:S(2)}) copy-start(s32[1,8]{1,0:T(1,128)} %param.10) | copy-start | bytes 100
  7.7 0.7 %copy-start.5 = (s32[36]{0:T(128)S(1)}, s32[36]{0:T(128)}, u32[]{:S(2)}) copy-start(s32[36]{0:T(128)} %constant.18.clone.table_ref) | copy-start | bytes 436
  12.9 7.6 %collective-permute-start.1 = (bf16[1040,128]{1,0:T(8,128)(2,1)S(1)}, bf16[1040,128]{1,0:T(8,128)(2,1)S(1)}, u32[]{:S(2)}, u32[]{:S(2)}) collective-permute-start(bf16[1040,128]{1,0:T(8,128)(2,1)S(1)} %pad_maximum_fusion.1), channel_id=1, source_target_pairs={{1,0},{0,1},{3,2},{2,3},{5,4},{4,5},{7,6},{6,7},{9,8},{8,9},{11,10... | collective-permute-start | bytes 798728 | tf_op jit(solution)/shard_map/ppermute | solution.py:328
  14.6 14.8 %collective-permute-start.5 = (bf16[8,128,128]{2,1,0:T(8,128)(2,1)S(1)}, bf16[8,128,128]{2,1,0:T(8,128)(2,1)S(1)}, u32[]{:S(2)}, u32[]{:S(2)}) collective-permute-start(bf16[8,128,128]{2,1,0:T(8,128)(2,1)S(1)} %slice.49), channel_id=1, source_target_pairs={{8,4},{10,6},{4,8},{6,10},{16,12},{18,14},{12,16},{14,18},{24,20},... | collective-permute-start | bytes 786440 | tf_op jit(solution)/shard_map/ppermute | solution.py:328
  16.6 12.9 %collective-permute-start.4 = (bf16[8,128,128]{2,1,0:T(8,128)(2,1)S(1)}, bf16[8,128,128]{2,1,0:T(8,128)(2,1)S(1)}, u32[]{:S(2)}, u32[]{:S(2)}) collective-permute-start(bf16[8,128,128]{2,1,0:T(8,128)(2,1)S(1)} %slice.48), channel_id=1, source_target_pairs={{12,4},{14,6},{0,8},{2,10},{20,12},{22,14},{8,16},{10,18},{28,20},... | collective-permute-start | bytes 786440 | tf_op jit(solution)/shard_map/ppermute | solution.py:328
  20.5 3.3 %collective-permute-start.6 = (bf16[16,128,128]{2,1,0:T(8,128)(2,1)S(1)}, bf16[16,128,128]{2,1,0:T(8,128)(2,1)S(1)}, u32[]{:S(2)}, u32[]{:S(2)}) collective-permute-start(bf16[16,128,128]{2,1,0:T(8,128)(2,1)S(1)} %collective-permute-done.3.refs_2_), channel_id=1, source_target_pairs={{2,0},{0,2},{6,4},{4,6},{10,8},{8,10},{14,12},{12,14},{18,16},{16,... | collective-permute-start | bytes 1572872 | tf_op jit(solution)/shard_map/ppermute | solution.py:328
  23.7 2.0 %collective-permute-start.7 = (bf16[16,128,128]{2,1,0:T(8,128)(2,1)S(1)}, bf16[16,128,128]{2,1,0:T(8,128)(2,1)S(1)}, u32[]{:S(2)}, u32[]{:S(2)}) collective-permute-start(bf16[16,128,128]{2,1,0:T(8,128)(2,1)S(1)} %slice.50), channel_id=1, source_target_pairs={{2,0},{0,2},{6,4},{4,6},{10,8},{8,10},{14,12},{12,14},{18,16},{16,... | collective-permute-start | bytes 1572872 | tf_op jit(solution)/shard_map/ppermute | solution.py:328
  29.5 2.0 %collective-permute-start.8 = (bf16[16,128,128]{2,1,0:T(8,128)(2,1)S(1)}, bf16[16,128,128]{2,1,0:T(8,128)(2,1)S(1)}, u32[]{:S(2)}, u32[]{:S(2)}) collective-permute-start(bf16[16,128,128]{2,1,0:T(8,128)(2,1)S(1)} %constant_dynamic-update-slice_fusion.refs_3_), channel_id=1, source_target_pairs={{2,0},{0,2},{6,4},{4,6},{10,8},{8,10},{14,12},{12,14},{18,16},{16,... | collective-permute-start | bytes 1572872 | tf_op jit(solution)/shard_map/ppermute | solution.py:328
  33.9 8.6 %collective-permute-start.9 = (bf16[8,128,128]{2,1,0:T(8,128)(2,1)S(1)}, bf16[8,128,128]{2,1,0:T(8,128)(2,1)S(1)}, u32[]{:S(2)}, u32[]{:S(2)}) collective-permute-start(bf16[8,128,128]{2,1,0:T(8,128)(2,1)S(1)} %get-tuple-element.41), channel_id=1, source_target_pairs={{1,0},{0,1},{3,2},{2,3},{5,4},{4,5},{7,6},{6,7},{9,8},{8,9},{11,10... | collective-permute-start | bytes 786440 | tf_op jit(solution)/shard_map/ppermute | solution.py:328
  35.2 7.3 %collective-permute-start.10 = (f32[8,2,128]{2,1,0:T(2,128)S(1)}, f32[8,2,128]{2,1,0:T(2,128)S(1)}, u32[]{:S(2)}, u32[]{:S(2)}) collective-permute-start(f32[8,2,128]{2,1,0:T(2,128)S(1)} %get-tuple-element.42), channel_id=1, source_target_pairs={{1,0},{0,1},{3,2},{2,3},{5,4},{4,5},{7,6},{6,7},{9,8},{8,9},{11,10... | collective-permute-start | bytes 24584 | tf_op jit(solution)/shard_map/ppermute | solution.py:328
where the time goes:
time: 43.5 us; the launch traced here: 43.4 us
  Pallas kernels  18 us (41%)
  starting transfers between devices  14 us (32%)
  waiting for transfers between devices  8.01 us (18%)
  local copies, waits for them, and re-layouts  2.95 us (7%)
    ppermute x11, starting transfers between devices, moved(): return lax.ppermute(block, axis, route)  14 us
    pallas_call x4, Pallas kernels, attend(): pl.pallas_call(functools.partial(phase_kernel, which, len(pieces), begins...  12.6 us
    ppermute x11, waiting for transfers between devices, moved(): return lax.ppermute(block, axis, route)  8.01 us
    pallas_call x1, Pallas kernels, work_lists(): pl.pallas_call(functools.partial(list_kernel, heads, length), in_specs=[S...  4.21 us
    unnamed x13, local copies, waits for them, and re-layouts  2.64 us
    pallas_call x1, Pallas kernels, merge(): pl.pallas_call(functools.partial(merge_kernel, len(parts)), in_specs=[VME...  0.91 us
  transfers between devices with their start and end apart: 11, of which 4 were waited for; matrix products, arithmetic and copies ran while one was open for 1% of the time, Pallas kernels for 33%

commit v1 on v0

--- a/solution.py
+++ b/solution.py
@@ -75,56 +75,59 @@
     )(*arrays)
 
 
-def list_kernel(heads, length, where_ref, lists_ref, live_ref, table_ref, ends, metas, places):
+def list_kernel(length, codes_ref, live_ref, ends, metas, places):
     tiles = live_ref.shape[0]
-    part_tiles = tiles // heads
-    frame, head = where_ref[0], where_ref[1]
-    base = lax.rem(frame, PLANE) * (2 * PLANE + 1) + PLANE - frame
-    targets = range(LISTS * heads)
-    for target in targets:
+    lists = ends.shape[0]
+    for target in range(lists):
         ends[target] = target * length
     for row in range(tiles):
-        part, inner = divmod(row, part_tiles)
-
-        def slot_step(slot, carry, row=row, part=part, inner=inner):
-            listed = lists_ref[row, slot]
-            within = listed & (tiles - 1)
-            rank = within >> int(math.log2(part_tiles))
-            spot = ((within & (part_tiles - 1)) * heads + head) * 2
-            entry = table_ref[base + (listed >> int(math.log2(tiles)))]
-            step = (rank - head) & (heads - 1)
-            turn = (rank - part) & (heads - 1)
-            own = turn == 0
-            query = (turn * part_tiles + inner) * heads + head
-            query = jnp.where(own, query, query - heads * part_tiles)
-            target = step * LISTS + 2 * (entry & 3) + jnp.where(own, 1, 0)
+
+        def slot_step(slot, carry, row=row):
+            code = codes_ref[row, slot]
+            target = (code >> 8) & 255
             at = ends[target]
-            places[at] = (entry >> 2) * (2 * tiles) + spot
-            metas[at >> 2] = query * 8 + (at & (GROUP - 1))
+            places[at] = code & 255
+            metas[at >> 2] = (code >> 16) + (at & (GROUP - 1))
             ends[target] = at + 1
             return carry
 
         lax.fori_loop(0, live_ref[row], slot_step, 0)
-        for target in targets:
+        for target in range(lists):
             at = ends[target]
             up = (at + GROUP - 1) & -GROUP
             filler = places[jnp.maximum(at - 1, 0)]
             for other in range(GROUP - 1):
-                spare = LISTS * heads * length
-                places[jnp.where(at + other < up, at + other, spare)] = filler
+                places[jnp.where(at + other < up, at + other, lists * length)] = filler
             ends[target] = up
-    for target in targets:
+    for target in range(lists):
         ends[target] = (ends[target] - target * length) >> 2
 
 
 def work_lists(frame, head, tile_lists, live_slots, heads):
     tiles, slots = tile_lists.shape
+    part_tiles = tiles // heads
     assert tiles & (tiles - 1) == 0 and heads & (heads - 1) == 0 and GROUP == 4
+    within = tile_lists & (tiles - 1)
+    rank = within >> int(math.log2(part_tiles))
+    spot = ((within & (part_tiles - 1)) * heads + head) * 2
+    table = shard_table()
+    key = lax.rem(frame, PLANE) * (2 * PLANE + 1) + PLANE - frame
+    key = (tile_lists >> int(math.log2(tiles))) + key
+    hit = key[..., None] == jnp.arange(table.size, dtype=jnp.int32)
+    entry = jnp.sum(jnp.where(hit, jnp.asarray(table), 0), axis=-1, dtype=jnp.int32)
+    row = jnp.arange(tiles, dtype=jnp.int32)[:, None]
+    turn = (rank - (row >> int(math.log2(part_tiles)))) & (heads - 1)
+    query = (turn * part_tiles + (row & (part_tiles - 1))) * heads + head
+    query = jnp.where(turn == 0, query, query - heads * part_tiles)
+    step = (rank - head) & (heads - 1)
+    target = step * LISTS + 2 * (entry & 3) + jnp.where(turn == 0, 1, 0)
+    place = (entry >> 2) * (2 * tiles) + spot
+    codes = place + target * 256 + query * (8 * 65536)
     length = tiles * (slots // GROUP + 1) * GROUP
     total = LISTS * heads * length
     ends, metas, places = pl.pallas_call(
-        functools.partial(list_kernel, heads, length),
-        in_specs=[SMEM] * 4,
+        functools.partial(list_kernel, length),
+        in_specs=[SMEM] * 2,
         out_specs=[SMEM] * 3,
         out_shape=[
             jax.ShapeDtypeStruct((LISTS * heads,), jnp.int32),
@@ -133,7 +136,7 @@
         ],
         compiler_params=params(4),
         cost_estimate=cost(),
-    )(jnp.stack((frame, head)), tile_lists, live_slots, jnp.asarray(shard_table()))
+    )(codes, live_slots)
     arrays = ends, metas, places[:total]
     return jnp.concatenate([array.reshape(heads, -1) for array in arrays], axis=1)
 
@@ -343,7 +346,7 @@
 
     own = as_tiles((key_vectors, value_vectors), (False, True))
     size = own.shape[0]
-    cut = size // 2
+    cut = size * 5 // 8
     across = moved(own, "frame", lambda i: i ^ 2)
     chip = jnp.concatenate((core_swap(own), own))
     level = moved(chip, "frame", lambda i: i - PLANE if i % 2 == 0 else i + PLANE)

time: 43.5 us -> 43.8 us (level)
  the two profiles are of different devices: /device:TPU:18 before, /device:TPU:0 now
where the time goes in v1:
time: 43.8 us; the launch traced here: 43.3 us
  starting transfers between devices  17.3 us (39%)
  Pallas kernels  16.2 us (37%)
  waiting for transfers between devices  5.18 us (12%)
  local copies, waits for them, and re-layouts  3.58 us (8%)
  other arithmetic  0.79 us (2%)
    ppermute x11, starting transfers between devices, moved(): return lax.ppermute(block, axis, route)  17.3 us
    pallas_call x4, Pallas kernels, attend(): pl.pallas_call(functools.partial(phase_kernel, which, len(pieces), begins...  11.7 us
    ppermute x11, waiting for transfers between devices, moved(): return lax.ppermute(block, axis, route)  5.18 us
    pallas_call x1, Pallas kernels, work_lists(): pl.pallas_call(functools.partial(list_kernel, length), in_specs=[SMEM] *...  3.39 us
    unnamed x13, local copies, waits for them, and re-layouts  3.12 us
    pallas_call x1, Pallas kernels, merge(): pl.pallas_call(functools.partial(merge_kernel, len(parts)), in_specs=[VME...  0.91 us
  transfers between devices with their start and end apart: 11, of which 5 were waited for; matrix products, arithmetic and copies ran while one was open for 3% of the time, Pallas kernels for 32%

profile of v1, /device:TPU:0, one launch (start us, length us, event | category | flops | bytes accessed | tf_op | source)
XLA Modules:
  0.0 43.3 jit_solution(6650942196266233640)
XLA Ops:
  0.0 1.0 %copy-done.1 = bf16[512,256]{1,0:T(8,128)(2,1)S(1)} copy-done((bf16[512,256]{1,0:T(8,128)(2,1)S(1)}, bf16[512,256]{1,0:T(8,128)(2,1)}, u32[]{:S(2)}) %copy-start.1) | copy-done | bytes 262168
  1.0 0.9 %copy-done.2 = bf16[512,256]{1,0:T(8,128)(2,1)S(1)} copy-done((bf16[512,256]{1,0:T(8,128)(2,1)S(1)}, bf16[512,256]{1,0:T(8,128)(2,1)}, u32[]{:S(2)}) %copy-start.2) | copy-done | bytes 262168
  1.9 0.1 shard_map.64
  2.1 0.5 %collective-permute-start = (bf16[16,128,128]{2,1,0:T(8,128)(2,1)S(1)}, bf16[16,128,128]{2,1,0:T(8,128)(2,1)S(1)}, u32[]{:S(2)}, u32[]{:S(2)}) collective-permute-start(bf16[16,128,128]{2,1,0:T(8,128)(2,1)S(1)} %shard_map.64), channel_id=1, source_target_pairs={{2,0},{0,2},{6,4},{4,6},{10,8},{8,10},{14,12},{12,14},{18,16},{16,... | collective-permute-start | bytes 1572872 | tf_op jit(solution)/shard_map/ppermute | solution.py:331
  2.6 2.6 %collective-permute-start.3 = (bf16[16,128,128]{2,1,0:T(8,128)(2,1)S(1)}, bf16[16,128,128]{2,1,0:T(8,128)(2,1)S(1)}, u32[]{:S(2)}, u32[]{:S(2)}) collective-permute-start(bf16[16,128,128]{2,1,0:T(8,128)(2,1)S(1)} %shard_map.64), channel_id=1, source_target_pairs={{4,0},{6,2},{0,4},{2,6},{12,8},{14,10},{8,12},{10,14},{20,16},{22,... | collective-permute-start | bytes 1572872 | tf_op jit(solution)/shard_map/ppermute | solution.py:331
  5.2 0.1 shard_map.66.q_ref
  5.3 0.1 pad_maximum_fusion.refs_0_
  5.4 3.7 %collective-permute-start.2 = (bf16[32,128,128]{2,1,0:T(8,128)(2,1)S(1)}, bf16[32,128,128]{2,1,0:T(8,128)(2,1)S(1)}, u32[]{:S(2)}, u32[]{:S(2)}) collective-permute-start(bf16[32,128,128]{2,1,0:T(8,128)(2,1)S(1)} %pad_maximum_fusion.refs_0_), channel_id=1, source_target_pairs={{10,2},{14,6},{0,8},{18,10},{4,12},{22,14},{8,16},{26,18},{12,20},... | collective-permute-start | bytes 3145736 | tf_op jit(solution)/shard_map/ppermute | solution.py:331
  9.2 0.1 copy.7
  9.3 0.6 %copy-done.5 = s32[36]{0:T(128)S(1)} copy-done((s32[36]{0:T(128)S(1)}, s32[36]{0:T(128)}, u32[]{:S(2)}) %copy-start.5) | copy-done | bytes 168
  9.8 0.5 %select_reduce_fusion = s32[8,20]{0,1:T(8,128)S(1)} fusion(s32[36]{0:T(128)S(1)} %copy-done.5, s32[8,20]{0,1:T(8,128)S(1)} %copy.7), kind=kLoop, calls=%fused_computation.2 | loop fusion | flops 17120 | bytes 1424 | tf_op jit(solution)/shard_map/reduce_sum | solution.py:117
  10.4 0.1 fusion.1.codes_ref
  10.5 0.6 %copy-done.3 = s32[1,8]{1,0:T(1,128)S(1)} copy-done((s32[1,8]{1,0:T(1,128)S(1)}, s32[1,8]{1,0:T(1,128)}, u32[]{:S(2)}) %copy-start.3) | copy-done | bytes 56
  11.1 3.4 %shard_map.65 = (s32[8]{0:T(128)S(1)}, s32[384]{0:T(512)S(1)}, s32[1537]{0:T(1024)S(1)}) custom-call(s32[8,20]{1,0:T(8,128)S(1)} %fusion.1.codes_ref, s32[8]{0:T(128)S(1)} %bitcast.18), custom_call_target="tpu_custom_call" | custom-call | tf_op jit(solution)/shard_map/pallas_call | solution.py:128
  14.5 0.1 reshape.36
  14.5 0.1 reshape.37
  14.8 1.6 %collective-permute-start.1 = (bf16[1040,128]{1,0:T(8,128)(2,1)S(1)}, bf16[1040,128]{1,0:T(8,128)(2,1)S(1)}, u32[]{:S(2)}, u32[]{:S(2)}) collective-permute-start(bf16[1040,128]{1,0:T(8,128)(2,1)S(1)} %pad_maximum_fusion.1), channel_id=1, source_target_pairs={{1,0},{0,1},{3,2},{2,3},{5,4},{4,5},{7,6},{6,7},{9,8},{8,9},{11,10... | collective-permute-start | bytes 798728 | tf_op jit(solution)/shard_map/ppermute | solution.py:331
  16.4 0.7 %collective-permute-start.5 = (bf16[6,128,128]{2,1,0:T(8,128)(2,1)S(1)}, bf16[6,128,128]{2,1,0:T(8,128)(2,1)S(1)}, u32[]{:S(2)}, u32[]{:S(2)}) collective-permute-start(bf16[6,128,128]{2,1,0:T(8,128)(2,1)S(1)} %slice.49), channel_id=1, source_target_pairs={{8,4},{10,6},{4,8},{6,10},{16,12},{18,14},{12,16},{14,18},{24,20},... | collective-permute-start | bytes 589832 | tf_op jit(solution)/shard_map/ppermute | solution.py:331
  17.0 0.6 %collective-permute-done.3.refs_2_ = bf16[16,128,128]{2,1,0:T(8,128)(2,1)S(1)} collective-permute-done((bf16[16,128,128]{2,1,0:T(8,128)(2,1)S(1)}, bf16[16,128,128]{2,1,0:T(8,128)(2,1)S(1)}, u32[]{:S(2)}, u32[]{:S(2)}) %collective-permute-start.3) | collective-permute-done | bytes 524320 | tf_op jit(solution)/shard_map/ppermute | solution.py:331
  17.7 5.5 %collective-permute-start.4 = (bf16[10,128,128]{2,1,0:T(8,128)(2,1)S(1)}, bf16[10,128,128]{2,1,0:T(8,128)(2,1)S(1)}, u32[]{:S(2)}, u32[]{:S(2)}) collective-permute-start(bf16[10,128,128]{2,1,0:T(8,128)(2,1)S(1)} %slice.48), channel_id=1, source_target_pairs={{12,4},{14,6},{0,8},{2,10},{20,12},{22,14},{8,16},{10,18},{28,20},... | collective-permute-start | bytes 983048 | tf_op jit(solution)/shard_map/ppermute | solution.py:331
  23.4 0.5 %collective-permute-start.7 = (bf16[16,128,128]{2,1,0:T(8,128)(2,1)S(1)}, bf16[16,128,128]{2,1,0:T(8,128)(2,1)S(1)}, u32[]{:S(2)}, u32[]{:S(2)}) collective-permute-start(bf16[16,128,128]{2,1,0:T(8,128)(2,1)S(1)} %slice.50), channel_id=1, source_target_pairs={{2,0},{0,2},{6,4},{4,6},{10,8},{8,10},{14,12},{12,14},{18,16},{16,... | collective-permute-start | bytes 1572872 | tf_op jit(solution)/shard_map/ppermute | solution.py:331
  24.0 1.2 %collective-permute-done.6.refs_3_ = bf16[16,128,128]{2,1,0:T(8,128)(2,1)S(1)} collective-permute-done((bf16[16,128,128]{2,1,0:T(8,128)(2,1)S(1)}, bf16[16,128,128]{2,1,0:T(8,128)(2,1)S(1)}, u32[]{:S(2)}, u32[]{:S(2)}) %collective-permute-start.6) | collective-permute-done | bytes 524320 | tf_op jit(solution)/shard_map/ppermute | solution.py:331
  25.2 0.7 %collective-permute-done.7.refs_4_ = bf16[16,128,128]{2,1,0:T(8,128)(2,1)S(1)} collective-permute-done((bf16[16,128,128]{2,1,0:T(8,128)(2,1)S(1)}, bf16[16,128,128]{2,1,0:T(8,128)(2,1)S(1)}, u32[]{:S(2)}, u32[]{:S(2)}) %collective-permute-start.7) | collective-permute-done | bytes 524320 | tf_op jit(solution)/shard_map/ppermute | solution.py:331
  25.9 4.7 %shard_map.67 = (f32[8,1,128]{2,1,0:T(1,128)S(1)}, f32[8,8,128]{2,1,0:T(8,128)S(1)}, f32[8,128,128]{2,1,0:T(8,128)S(1)}) custom-call(s32[2,964]{1,0:T(2,128)S(1)} %pad_add_fusion.1.lists, bf16[8,128,128]{2,1,0:T(8,128)(2,1)S(1)} %bitcast.15, bf16[32,128,128]{2,1,0:T(8,128)(2,1)S(1)} %pad_maximum_fusion.refs_0_, ...), custom_call_target="tpu_custom_call" | custom-call | tf_op jit(solution)/shard_map/pallas_call | solution.py:286
  30.8 1.9 %collective-permute-done.8.refs_4_ = bf16[16,128,128]{2,1,0:T(8,128)(2,1)S(1)} collective-permute-done((bf16[16,128,128]{2,1,0:T(8,128)(2,1)S(1)}, bf16[16,128,128]{2,1,0:T(8,128)(2,1)S(1)}, u32[]{:S(2)}, u32[]{:S(2)}) %collective-permute-start.8) | collective-permute-done | bytes 524320 | tf_op jit(solution)/shard_map/ppermute | solution.py:331
  32.7 1.1 %shard_map.68 = (bf16[8,128,128]{2,1,0:T(8,128)(2,1)S(1)}, f32[8,2,128]{2,1,0:T(2,128)S(1)}) custom-call(s32[2,964]{1,0:T(2,128)S(1)} %pad_add_fusion.1.lists, bf16[8,128,128]{2,1,0:T(8,128)(2,1)S(1)} %bitcast.16, f32[8,1,128]{2,1,0:T(1,128)S(1)} %get-tuple-element.36.refs_0_, f32[8,8,128]{2,1,0:T(8,128)S(1)} %get-tuple-element.37.refs_1_, ...), custom_call_target="tpu_custom_call" | custom-call | tf_op jit(solution)/shard_map/pallas_call | solution.py:286
  33.8 0.2 collective-permute-start.9
  34.0 1.9 %collective-permute-start.10 = (f32[8,2,128]{2,1,0:T(2,128)S(1)}, f32[8,2,128]{2,1,0:T(2,128)S(1)}, u32[]{:S(2)}, u32[]{:S(2)}) collective-permute-start(f32[8,2,128]{2,1,0:T(2,128)S(1)} %get-tuple-element.42), channel_id=1, source_target_pairs={{1,0},{0,1},{3,2},{2,3},{5,4},{4,5},{7,6},{6,7},{9,8},{8,9},{11,10... | collective-permute-start | bytes 24584 | tf_op jit(solution)/shard_map/ppermute | solution.py:331
  35.9 4.7 %shard_map.69 = (f32[8,1,128]{2,1,0:T(1,128)S(1)}, f32[8,8,128]{2,1,0:T(8,128)S(1)}, f32[8,128,128]{2,1,0:T(8,128)S(1)}) custom-call(s32[2,964]{1,0:T(2,128)S(1)} %pad_add_fusion.1.lists, bf16[8,128,128]{2,1,0:T(8,128)(2,1)S(1)} %shard_map.66.q_ref, bf16[32,128,128]{2,1,0:T(8,128)(2,1)S(1)} %pad_maximum_fusion.refs_0_, ...), custom_call_target="tpu_custom_call" | custom-call | tf_op jit(solution)/shard_map/pallas_call | solution.py:286
  40.6 1.2 %shard_map.70 = (bf16[8,128,128]{2,1,0:T(8,128)(2,1)S(1)}, f32[8,2,128]{2,1,0:T(2,128)S(1)}) custom-call(s32[2,964]{1,0:T(2,128)S(1)} %pad_add_fusion.1.lists, bf16[8,128,128]{2,1,0:T(8,128)(2,1)S(1)} %shard_map.66.q_ref, f32[8,1,128]{2,1,0:T(1,128)S(1)} %get-tuple-element.44.refs_0_, f32[8,8,128]{2,1,0:T(8,128)S(1)} %get-tuple-element.45.refs_1_, ...), custom_call_target="tpu_custom_call" | custom-call | tf_op jit(solution)/shard_map/pallas_call | solution.py:286
  41.8 0.7 %collective-permute-done.10.refs_3_ = f32[8,2,128]{2,1,0:T(2,128)S(1)} collective-permute-done((f32[8,2,128]{2,1,0:T(2,128)S(1)}, f32[8,2,128]{2,1,0:T(2,128)S(1)}, u32[]{:S(2)}, u32[]{:S(2)}) %collective-permute-start.10) | collective-permute-done | bytes 8224 | tf_op jit(solution)/shard_map/ppermute | solution.py:331
  42.4 0.9 %shard_map.71 = bf16[512,256]{1,0:T(8,128)(2,1)} custom-call(bf16[8,128,128]{2,1,0:T(8,128)(2,1)S(1)} %get-tuple-element.47.refs_0_, f32[8,2,128]{2,1,0:T(2,128)S(1)} %get-tuple-element.48.refs_1_, bf16[8,128,128]{2,1,0:T(8,128)(2,1)S(1)} %collective-permute-done.9.refs_2_, f32[8,2,128]{2,1,0:T(2,128)S(1)} %collective-permute-done.10.refs_3_), custom_call_target="tpu_custom_call" | custom-call | tf_op jit(solution)/shard_map/pallas_call | solution.py:319
  (33 shorter events, 0.6 us)
Async XLA Ops:
  0.0 5.2 %copy-start = (bf16[512,256]{1,0:T(8,128)(2,1)S(1)}, bf16[512,256]{1,0:T(8,128)(2,1)}, u32[]{:S(2)}) copy-start(bf16[512,256]{1,0:T(8,128)(2,1)} %refs_0_.3) | copy-start | bytes 786436
  0.0 1.0 %copy-start.1 = (bf16[512,256]{1,0:T(8,128)(2,1)S(1)}, bf16[512,256]{1,0:T(8,128)(2,1)}, u32[]{:S(2)}) copy-start(bf16[512,256]{1,0:T(8,128)(2,1)} %refs_0_.2) | copy-start | bytes 786436
  1.0 0.9 %copy-start.2 = (bf16[512,256]{1,0:T(8,128)(2,1)S(1)}, bf16[512,256]{1,0:T(8,128)(2,1)}, u32[]{:S(2)}) copy-start(bf16[512,256]{1,0:T(8,128)(2,1)} %refs_1_.1) | copy-start | bytes 786436
  2.1 3.2 %collective-permute-start = (bf16[16,128,128]{2,1,0:T(8,128)(2,1)S(1)}, bf16[16,128,128]{2,1,0:T(8,128)(2,1)S(1)}, u32[]{:S(2)}, u32[]{:S(2)}) collective-permute-start(bf16[16,128,128]{2,1,0:T(8,128)(2,1)S(1)} %shard_map.64), channel_id=1, source_target_pairs={{2,0},{0,2},{6,4},{4,6},{10,8},{8,10},{14,12},{12,14},{18,16},{16,... | collective-permute-start | bytes 1572872 | tf_op jit(solution)/shard_map/ppermute | solution.py:331
  2.6 15.1 %collective-permute-start.3 = (bf16[16,128,128]{2,1,0:T(8,128)(2,1)S(1)}, bf16[16,128,128]{2,1,0:T(8,128)(2,1)S(1)}, u32[]{:S(2)}, u32[]{:S(2)}) collective-permute-start(bf16[16,128,128]{2,1,0:T(8,128)(2,1)S(1)} %shard_map.64), channel_id=1, source_target_pairs={{4,0},{6,2},{0,4},{2,6},{12,8},{14,10},{8,12},{10,14},{20,16},{22,... | collective-permute-start | bytes 1572872 | tf_op jit(solution)/shard_map/ppermute | solution.py:331
  5.3 3.8 %copy-start.4 = (s32[1,8,20]{2,1,0:T(8,128)S(1)}, s32[1,8,20]{2,1,0:T(8,128)}, u32[]{:S(2)}) copy-start(s32[1,8,20]{2,1,0:T(8,128)} %param.9) | copy-start | bytes 1924
  5.4 17.9 %collective-permute-start.2 = (bf16[32,128,128]{2,1,0:T(8,128)(2,1)S(1)}, bf16[32,128,128]{2,1,0:T(8,128)(2,1)S(1)}, u32[]{:S(2)}, u32[]{:S(2)}) collective-permute-start(bf16[32,128,128]{2,1,0:T(8,128)(2,1)S(1)} %pad_maximum_fusion.refs_0_), channel_id=1, source_target_pairs={{10,2},{14,6},{0,8},{18,10},{4,12},{22,14},{8,16},{26,18},{12,20},... | collective-permute-start | bytes 3145736 | tf_op jit(solution)/shard_map/ppermute | solution.py:331
  9.2 0.7 %copy-start.5 = (s32[36]{0:T(128)S(1)}, s32[36]{0:T(128)}, u32[]{:S(2)}) copy-start(s32[36]{0:T(128)} %constant.15.clone) | copy-start | bytes 436
  10.4 0.7 %copy-start.3 = (s32[1,8]{1,0:T(1,128)S(1)}, s32[1,8]{1,0:T(1,128)}, u32[]{:S(2)}) copy-start(s32[1,8]{1,0:T(1,128)} %param.10) | copy-start | bytes 100
  14.8 8.5 %collective-permute-start.1 = (bf16[1040,128]{1,0:T(8,128)(2,1)S(1)}, bf16[1040,128]{1,0:T(8,128)(2,1)S(1)}, u32[]{:S(2)}, u32[]{:S(2)}) collective-permute-start(bf16[1040,128]{1,0:T(8,128)(2,1)S(1)} %pad_maximum_fusion.1), channel_id=1, source_target_pairs={{1,0},{0,1},{3,2},{2,3},{5,4},{4,5},{7,6},{6,7},{9,8},{8,9},{11,10... | collective-permute-start | bytes 798728 | tf_op jit(solution)/shard_map/ppermute | solution.py:331
  16.4 14.3 %collective-permute-start.5 = (bf16[6,128,128]{2,1,0:T(8,128)(2,1)S(1)}, bf16[6,128,128]{2,1,0:T(8,128)(2,1)S(1)}, u32[]{:S(2)}, u32[]{:S(2)}) collective-permute-start(bf16[6,128,128]{2,1,0:T(8,128)(2,1)S(1)} %slice.49), channel_id=1, source_target_pairs={{8,4},{10,6},{4,8},{6,10},{16,12},{18,14},{12,16},{14,18},{24,20},... | collective-permute-start | bytes 589832 | tf_op jit(solution)/shard_map/ppermute | solution.py:331
  17.7 12.9 %collective-permute-start.4 = (bf16[10,128,128]{2,1,0:T(8,128)(2,1)S(1)}, bf16[10,128,128]{2,1,0:T(8,128)(2,1)S(1)}, u32[]{:S(2)}, u32[]{:S(2)}) collective-permute-start(bf16[10,128,128]{2,1,0:T(8,128)(2,1)S(1)} %slice.48), channel_id=1, source_target_pairs={{12,4},{14,6},{0,8},{2,10},{20,12},{22,14},{8,16},{10,18},{28,20},... | collective-permute-start | bytes 983048 | tf_op jit(solution)/shard_map/ppermute | solution.py:331
  23.2 2.0 %collective-permute-start.6 = (bf16[16,128,128]{2,1,0:T(8,128)(2,1)S(1)}, bf16[16,128,128]{2,1,0:T(8,128)(2,1)S(1)}, u32[]{:S(2)}, u32[]{:S(2)}) collective-permute-start(bf16[16,128,128]{2,1,0:T(8,128)(2,1)S(1)} %collective-permute-done.3.refs_2_), channel_id=1, source_target_pairs={{2,0},{0,2},{6,4},{4,6},{10,8},{8,10},{14,12},{12,14},{18,16},{16,... | collective-permute-start | bytes 1572872 | tf_op jit(solution)/shard_map/ppermute | solution.py:331
  23.4 2.6 %collective-permute-start.7 = (bf16[16,128,128]{2,1,0:T(8,128)(2,1)S(1)}, bf16[16,128,128]{2,1,0:T(8,128)(2,1)S(1)}, u32[]{:S(2)}, u32[]{:S(2)}) collective-permute-start(bf16[16,128,128]{2,1,0:T(8,128)(2,1)S(1)} %slice.50), channel_id=1, source_target_pairs={{2,0},{0,2},{6,4},{4,6},{10,8},{8,10},{14,12},{12,14},{18,16},{16,... | collective-permute-start | bytes 1572872 | tf_op jit(solution)/shard_map/ppermute | solution.py:331
  30.7 2.0 %collective-permute-start.8 = (bf16[16,128,128]{2,1,0:T(8,128)(2,1)S(1)}, bf16[16,128,128]{2,1,0:T(8,128)(2,1)S(1)}, u32[]{:S(2)}, u32[]{:S(2)}) collective-permute-start(bf16[16,128,128]{2,1,0:T(8,128)(2,1)S(1)} %constant_dynamic-update-slice_fusion.refs_3_), channel_id=1, source_target_pairs={{2,0},{0,2},{6,4},{4,6},{10,8},{8,10},{14,12},{12,14},{18,16},{16,... | collective-permute-start | bytes 1572872 | tf_op jit(solution)/shard_map/ppermute | solution.py:331
  33.8 8.6 %collective-permute-start.9 = (bf16[8,128,128]{2,1,0:T(8,128)(2,1)S(1)}, bf16[8,128,128]{2,1,0:T(8,128)(2,1)S(1)}, u32[]{:S(2)}, u32[]{:S(2)}) collective-permute-start(bf16[8,128,128]{2,1,0:T(8,128)(2,1)S(1)} %get-tuple-element.41), channel_id=1, source_target_pairs={{1,0},{0,1},{3,2},{2,3},{5,4},{4,5},{7,6},{6,7},{9,8},{8,9},{11,10... | collective-permute-start | bytes 786440 | tf_op jit(solution)/shard_map/ppermute | solution.py:331
  34.0 8.4 %collective-permute-start.10 = (f32[8,2,128]{2,1,0:T(2,128)S(1)}, f32[8,2,128]{2,1,0:T(2,128)S(1)}, u32[]{:S(2)}, u32[]{:S(2)}) collective-permute-start(f32[8,2,128]{2,1,0:T(2,128)S(1)} %get-tuple-element.42), channel_id=1, source_target_pairs={{1,0},{0,1},{3,2},{2,3},{5,4},{4,5},{7,6},{6,7},{9,8},{8,9},{11,10... | collective-permute-start | bytes 24584 | tf_op jit(solution)/shard_map/ppermute | solution.py:331

commit v2 on v1

--- a/solution.py
+++ b/solution.py
@@ -123,7 +123,7 @@
     target = step * LISTS + 2 * (entry & 3) + jnp.where(turn == 0, 1, 0)
     place = (entry >> 2) * (2 * tiles) + spot
     codes = place + target * 256 + query * (8 * 65536)
-    length = tiles * (slots // GROUP + 1) * GROUP
+    length = max(part_tiles, tiles - part_tiles) * -(-slots // GROUP) * GROUP
     total = LISTS * heads * length
     ends, metas, places = pl.pallas_call(
         functools.partial(list_kernel, length),
@@ -346,7 +346,7 @@
 
     own = as_tiles((key_vectors, value_vectors), (False, True))
     size = own.shape[0]
-    cut = size * 5 // 8
+    cut = size * 9 // 16
     across = moved(own, "frame", lambda i: i ^ 2)
     chip = jnp.concatenate((core_swap(own), own))
     level = moved(chip, "frame", lambda i: i - PLANE if i % 2 == 0 else i + PLANE)
@@ -370,9 +370,10 @@
     straight = moved(own[cut:], "frame", lambda i: i - 2 if i % PLANE < 2 else i + 2)
     near = [chip, level, across, core_swap(across), core_swap(level[:size])]
     state = attend(by_head, 0, q_rest, None, near, False)
-    far_z, straight, state = lax.optimization_barrier((far_z, straight, state))
-    far = jnp.concatenate((far_z, straight))
-    far = [far, core_swap(far)]
+    straight, state = lax.optimization_barrier((straight, state))
+    swapped = core_swap(straight)
+    far_z, swapped = lax.optimization_barrier((far_z, swapped))
+    far = [far_z, straight, core_swap(far_z), swapped]
     rest = attend(by_head, 2, q_rest, state, far, True)
     parts = [None]
     for step in range(1, heads):

time: 43.8 us -> 43.5 us (level)
  the two profiles are of different devices: /device:TPU:0 before, /device:TPU:18 now
where the time goes in v2:
time: 43.5 us; the launch traced here: 43.4 us
  starting transfers between devices  16.2 us (37%)
  Pallas kernels  12.9 us (30%)
  waiting for transfers between devices  9.72 us (22%)
  local copies, waits for them, and re-layouts  3.6 us (8%)
  other arithmetic  0.8 us (2%)
    ppermute x12, starting transfers between devices, moved(): return lax.ppermute(block, axis, route)  16.2 us
    ppermute x12, waiting for transfers between devices, moved(): return lax.ppermute(block, axis, route)  9.72 us
    pallas_call x4, Pallas kernels, attend(): pl.pallas_call(functools.partial(phase_kernel, which, len(pieces), begins...  9.53 us
    unnamed x12, local copies, waits for them, and re-layouts  3.1 us
    pallas_call x1, Pallas kernels, work_lists(): pl.pallas_call(functools.partial(list_kernel, length), in_specs=[SMEM] *...  2.18 us
    pallas_call x1, Pallas kernels, merge(): pl.pallas_call(functools.partial(merge_kernel, len(parts)), in_specs=[VME...  0.91 us
  transfers between devices with their start and end apart: 12, of which 6 were waited for; matrix products, arithmetic and copies ran while one was open for 3% of the time, Pallas kernels for 23%

profile of v2, /device:TPU:18, one launch (start us, length us, event | category | flops | bytes accessed | tf_op | source)
XLA Modules:
  0.0 43.4 jit_solution(2974616617127086725)
XLA Ops:
  0.0 1.0 %copy-done.1 = bf16[512,256]{1,0:T(8,128)(2,1)S(1)} copy-done((bf16[512,256]{1,0:T(8,128)(2,1)S(1)}, bf16[512,256]{1,0:T(8,128)(2,1)}, u32[]{:S(2)}) %copy-start.1) | copy-done | bytes 262168
  1.0 0.9 %copy-done.2 = bf16[512,256]{1,0:T(8,128)(2,1)S(1)} copy-done((bf16[512,256]{1,0:T(8,128)(2,1)S(1)}, bf16[512,256]{1,0:T(8,128)(2,1)}, u32[]{:S(2)}) %copy-start.2) | copy-done | bytes 262168
  1.9 0.1 shard_map.64
  2.2 0.6 %collective-permute-start.4 = (bf16[16,128,128]{2,1,0:T(8,128)(2,1)S(1)}, bf16[16,128,128]{2,1,0:T(8,128)(2,1)S(1)}, u32[]{:S(2)}, u32[]{:S(2)}) collective-permute-start(bf16[16,128,128]{2,1,0:T(8,128)(2,1)S(1)} %shard_map.64), channel_id=1, source_target_pairs={{4,0},{6,2},{0,4},{2,6},{12,8},{14,10},{8,12},{10,14},{20,16},{22,... | collective-permute-start | bytes 1572872 | tf_op jit(solution)/shard_map/ppermute | solution.py:331
  2.8 0.1 shard_map.66.q_ref
  2.9 1.2 %collective-permute-done = bf16[16,128,128]{2,1,0:T(8,128)(2,1)S(1)} collective-permute-done((bf16[16,128,128]{2,1,0:T(8,128)(2,1)S(1)}, bf16[16,128,128]{2,1,0:T(8,128)(2,1)S(1)}, u32[]{:S(2)}, u32[]{:S(2)}) %collective-permute-start) | collective-permute-done | bytes 524320 | tf_op jit(solution)/shard_map/ppermute | solution.py:331
  4.1 0.1 pad_maximum_fusion.refs_0_
  4.1 3.5 %collective-permute-start.2 = (bf16[32,128,128]{2,1,0:T(8,128)(2,1)S(1)}, bf16[32,128,128]{2,1,0:T(8,128)(2,1)S(1)}, u32[]{:S(2)}, u32[]{:S(2)}) collective-permute-start(bf16[32,128,128]{2,1,0:T(8,128)(2,1)S(1)} %pad_maximum_fusion.refs_0_), channel_id=1, source_target_pairs={{10,2},{14,6},{0,8},{18,10},{4,12},{22,14},{8,16},{26,18},{12,20},... | collective-permute-start | bytes 3145736 | tf_op jit(solution)/shard_map/ppermute | solution.py:331
  7.7 0.1 copy.7
  7.8 0.6 %copy-done.5 = s32[36]{0:T(128)S(1)} copy-done((s32[36]{0:T(128)S(1)}, s32[36]{0:T(128)}, u32[]{:S(2)}) %copy-start.5) | copy-done | bytes 168
  8.3 0.5 %select_reduce_fusion = s32[8,20]{0,1:T(8,128)S(1)} fusion(s32[36]{0:T(128)S(1)} %copy-done.5, s32[8,20]{0,1:T(8,128)S(1)} %copy.7), kind=kLoop, calls=%fused_computation.2 | loop fusion | flops 17120 | bytes 1424 | tf_op jit(solution)/shard_map/reduce_sum | solution.py:117
  8.9 0.1 fusion.3.codes_ref
  9.0 0.6 %copy-done.3 = s32[1,8]{1,0:T(1,128)S(1)} copy-done((s32[1,8]{1,0:T(1,128)S(1)}, s32[1,8]{1,0:T(1,128)}, u32[]{:S(2)}) %copy-start.3) | copy-done | bytes 56
  9.5 2.2 %shard_map.65 = (s32[8]{0:T(128)S(1)}, s32[160]{0:T(256)S(1)}, s32[641]{0:T(1024)S(1)}) custom-call(s32[8,20]{1,0:T(8,128)S(1)} %fusion.3.codes_ref, s32[8]{0:T(128)S(1)} %bitcast.18), custom_call_target="tpu_custom_call" | custom-call | tf_op jit(solution)/shard_map/pallas_call | solution.py:128
  11.7 0.1 reshape.36
  11.8 0.1 reshape.37
  12.1 2.7 %collective-permute-start.1 = (bf16[1040,128]{1,0:T(8,128)(2,1)S(1)}, bf16[1040,128]{1,0:T(8,128)(2,1)S(1)}, u32[]{:S(2)}, u32[]{:S(2)}) collective-permute-start(bf16[1040,128]{1,0:T(8,128)(2,1)S(1)} %pad_maximum_fusion.1), channel_id=1, source_target_pairs={{1,0},{0,1},{3,2},{2,3},{5,4},{4,5},{7,6},{6,7},{9,8},{8,9},{11,10... | collective-permute-start | bytes 798728 | tf_op jit(solution)/shard_map/ppermute | solution.py:331
  14.8 1.9 %collective-permute-start.3 = (bf16[7,128,128]{2,1,0:T(8,128)(2,1)S(1)}, bf16[7,128,128]{2,1,0:T(8,128)(2,1)S(1)}, u32[]{:S(2)}, u32[]{:S(2)}) collective-permute-start(bf16[7,128,128]{2,1,0:T(8,128)(2,1)S(1)} %slice.48), channel_id=1, source_target_pairs={{8,4},{10,6},{4,8},{6,10},{16,12},{18,14},{12,16},{14,18},{24,20},... | collective-permute-start | bytes 688136 | tf_op jit(solution)/shard_map/ppermute | solution.py:331
  16.8 3.8 %collective-permute-start.7 = (bf16[9,128,128]{2,1,0:T(8,128)(2,1)S(1)}, bf16[9,128,128]{2,1,0:T(8,128)(2,1)S(1)}, u32[]{:S(2)}, u32[]{:S(2)}) collective-permute-start(bf16[9,128,128]{2,1,0:T(8,128)(2,1)S(1)} %slice.50), channel_id=1, source_target_pairs={{12,4},{14,6},{0,8},{2,10},{20,12},{22,14},{8,16},{10,18},{28,20},... | collective-permute-start | bytes 884744 | tf_op jit(solution)/shard_map/ppermute | solution.py:331
  20.7 2.6 %collective-permute-done.2.refs_1_ = bf16[32,128,128]{2,1,0:T(8,128)(2,1)S(1)} collective-permute-done((bf16[32,128,128]{2,1,0:T(8,128)(2,1)S(1)}, bf16[32,128,128]{2,1,0:T(8,128)(2,1)S(1)}, u32[]{:S(2)}, u32[]{:S(2)}) %collective-permute-start.2) | collective-permute-done | bytes 1048608 | tf_op jit(solution)/shard_map/ppermute | solution.py:331
  23.5 1.8 %collective-permute-done.6.refs_4_ = bf16[16,128,128]{2,1,0:T(8,128)(2,1)S(1)} collective-permute-done((bf16[16,128,128]{2,1,0:T(8,128)(2,1)S(1)}, bf16[16,128,128]{2,1,0:T(8,128)(2,1)S(1)}, u32[]{:S(2)}, u32[]{:S(2)}) %collective-permute-start.6) | collective-permute-done | bytes 524320 | tf_op jit(solution)/shard_map/ppermute | solution.py:331
  25.3 2.7 %shard_map.67 = (f32[8,1,128]{2,1,0:T(1,128)S(1)}, f32[8,8,128]{2,1,0:T(8,128)S(1)}, f32[8,128,128]{2,1,0:T(8,128)S(1)}) custom-call(s32[2,404]{1,0:T(2,128)S(1)} %pad_add_fusion.1.lists, bf16[8,128,128]{2,1,0:T(8,128)(2,1)S(1)} %bitcast.15, bf16[32,128,128]{2,1,0:T(8,128)(2,1)S(1)} %pad_maximum_fusion.refs_0_, ...), custom_call_target="tpu_custom_call" | custom-call | tf_op jit(solution)/shard_map/pallas_call | solution.py:286
  28.1 0.8 %collective-permute-start.8 = (bf16[7,128,128]{2,1,0:T(8,128)(2,1)S(1)}, bf16[7,128,128]{2,1,0:T(8,128)(2,1)S(1)}, u32[]{:S(2)}, u32[]{:S(2)}) collective-permute-start(bf16[7,128,128]{2,1,0:T(8,128)(2,1)S(1)} %collective-permute-done.3.refs_4_), channel_id=1, source_target_pairs={{2,0},{0,2},{6,4},{4,6},{10,8},{8,10},{14,12},{12,14},{18,16},{16,... | collective-permute-start | bytes 688136 | tf_op jit(solution)/shard_map/ppermute | solution.py:331
  28.9 1.1 %collective-permute-done.8.refs_6_ = bf16[7,128,128]{2,1,0:T(8,128)(2,1)S(1)} collective-permute-done((bf16[7,128,128]{2,1,0:T(8,128)(2,1)S(1)}, bf16[7,128,128]{2,1,0:T(8,128)(2,1)S(1)}, u32[]{:S(2)}, u32[]{:S(2)}) %collective-permute-start.8) | collective-permute-done | bytes 229408 | tf_op jit(solution)/shard_map/ppermute | solution.py:331
  30.0 0.4 collective-permute-start.9
  30.4 1.2 %collective-permute-done.9.refs_5_ = bf16[9,128,128]{2,1,0:T(8,128)(2,1)S(1)} collective-permute-done((bf16[9,128,128]{2,1,0:T(8,128)(2,1)S(1)}, bf16[9,128,128]{2,1,0:T(8,128)(2,1)S(1)}, u32[]{:S(2)}, u32[]{:S(2)}) %collective-permute-start.9) | collective-permute-done | bytes 294944 | tf_op jit(solution)/shard_map/ppermute | solution.py:331
  31.6 1.7 %shard_map.68 = (bf16[8,128,128]{2,1,0:T(8,128)(2,1)S(1)}, f32[8,2,128]{2,1,0:T(2,128)S(1)}) custom-call(s32[2,404]{1,0:T(2,128)S(1)} %pad_add_fusion.1.lists, bf16[8,128,128]{2,1,0:T(8,128)(2,1)S(1)} %bitcast.16, f32[8,1,128]{2,1,0:T(1,128)S(1)} %get-tuple-element.37.refs_0_, f32[8,8,128]{2,1,0:T(8,128)S(1)} %get-tuple-element.38.refs_1_, ...), custom_call_target="tpu_custom_call" | custom-call | tf_op jit(solution)/shard_map/pallas_call | solution.py:286
  33.3 2.2 %collective-permute-start.10 = (bf16[8,128,128]{2,1,0:T(8,128)(2,1)S(1)}, bf16[8,128,128]{2,1,0:T(8,128)(2,1)S(1)}, u32[]{:S(2)}, u32[]{:S(2)}) collective-permute-start(bf16[8,128,128]{2,1,0:T(8,128)(2,1)S(1)} %get-tuple-element.43), channel_id=1, source_target_pairs={{1,0},{0,1},{3,2},{2,3},{5,4},{4,5},{7,6},{6,7},{9,8},{8,9},{11,10... | collective-permute-start | bytes 786440 | tf_op jit(solution)/shard_map/ppermute | solution.py:331
  35.6 3.0 %shard_map.69 = (f32[8,1,128]{2,1,0:T(1,128)S(1)}, f32[8,8,128]{2,1,0:T(8,128)S(1)}, f32[8,128,128]{2,1,0:T(8,128)S(1)}) custom-call(s32[2,404]{1,0:T(2,128)S(1)} %pad_add_fusion.1.lists, bf16[8,128,128]{2,1,0:T(8,128)(2,1)S(1)} %shard_map.66.q_ref, bf16[32,128,128]{2,1,0:T(8,128)(2,1)S(1)} %pad_maximum_fusion.refs_0_, ...), custom_call_target="tpu_custom_call" | custom-call | tf_op jit(solution)/shard_map/pallas_call | solution.py:286
  38.6 2.0 %shard_map.70 = (bf16[8,128,128]{2,1,0:T(8,128)(2,1)S(1)}, f32[8,2,128]{2,1,0:T(2,128)S(1)}) custom-call(s32[2,404]{1,0:T(2,128)S(1)} %pad_add_fusion.1.lists, bf16[8,128,128]{2,1,0:T(8,128)(2,1)S(1)} %shard_map.66.q_ref, f32[8,1,128]{2,1,0:T(1,128)S(1)} %get-tuple-element.46.refs_0_, f32[8,8,128]{2,1,0:T(8,128)S(1)} %get-tuple-element.47.refs_1_, ...), custom_call_target="tpu_custom_call" | custom-call | tf_op jit(solution)/shard_map/pallas_call | solution.py:286
  40.7 1.8 %collective-permute-done.11.refs_3_ = f32[8,2,128]{2,1,0:T(2,128)S(1)} collective-permute-done((f32[8,2,128]{2,1,0:T(2,128)S(1)}, f32[8,2,128]{2,1,0:T(2,128)S(1)}, u32[]{:S(2)}, u32[]{:S(2)}) %collective-permute-start.11) | collective-permute-done | bytes 8224 | tf_op jit(solution)/shard_map/ppermute | solution.py:331
  42.5 0.9 %shard_map.71 = bf16[512,256]{1,0:T(8,128)(2,1)} custom-call(bf16[8,128,128]{2,1,0:T(8,128)(2,1)S(1)} %get-tuple-element.49.refs_0_, f32[8,2,128]{2,1,0:T(2,128)S(1)} %get-tuple-element.50.refs_1_, bf16[8,128,128]{2,1,0:T(8,128)(2,1)S(1)} %collective-permute-done.10.refs_2_, f32[8,2,128]{2,1,0:T(2,128)S(1)} %collective-permute-done.11.refs_3_), custom_call_target="tpu_custom_call" | custom-call | tf_op jit(solution)/shard_map/pallas_call | solution.py:319
  (34 shorter events, 0.7 us)
Async XLA Ops:
  0.0 2.8 %copy-start = (bf16[512,256]{1,0:T(8,128)(2,1)S(1)}, bf16[512,256]{1,0:T(8,128)(2,1)}, u32[]{:S(2)}) copy-start(bf16[512,256]{1,0:T(8,128)(2,1)} %refs_0_.3) | copy-start | bytes 786436
  0.0 1.0 %copy-start.1 = (bf16[512,256]{1,0:T(8,128)(2,1)S(1)}, bf16[512,256]{1,0:T(8,128)(2,1)}, u32[]{:S(2)}) copy-start(bf16[512,256]{1,0:T(8,128)(2,1)} %refs_0_.2) | copy-start | bytes 786436
  1.0 0.9 %copy-start.2 = (bf16[512,256]{1,0:T(8,128)(2,1)S(1)}, bf16[512,256]{1,0:T(8,128)(2,1)}, u32[]{:S(2)}) copy-start(bf16[512,256]{1,0:T(8,128)(2,1)} %refs_1_.1) | copy-start | bytes 786436
  2.1 2.0 %collective-permute-start = (bf16[16,128,128]{2,1,0:T(8,128)(2,1)S(1)}, bf16[16,128,128]{2,1,0:T(8,128)(2,1)S(1)}, u32[]{:S(2)}, u32[]{:S(2)}) collective-permute-start(bf16[16,128,128]{2,1,0:T(8,128)(2,1)S(1)} %shard_map.64), channel_id=1, source_target_pairs={{2,0},{0,2},{6,4},{4,6},{10,8},{8,10},{14,12},{12,14},{18,16},{16,... | collective-permute-start | bytes 1572872 | tf_op jit(solution)/shard_map/ppermute | solution.py:331
  2.2 14.6 %collective-permute-start.4 = (bf16[16,128,128]{2,1,0:T(8,128)(2,1)S(1)}, bf16[16,128,128]{2,1,0:T(8,128)(2,1)S(1)}, u32[]{:S(2)}, u32[]{:S(2)}) collective-permute-start(bf16[16,128,128]{2,1,0:T(8,128)(2,1)S(1)} %shard_map.64), channel_id=1, source_target_pairs={{4,0},{6,2},{0,4},{2,6},{12,8},{14,10},{8,12},{10,14},{20,16},{22,... | collective-permute-start | bytes 1572872 | tf_op jit(solution)/shard_map/ppermute | solution.py:331
  4.0 3.6 %copy-start.4 = (s32[1,8,20]{2,1,0:T(8,128)S(1)}, s32[1,8,20]{2,1,0:T(8,128)}, u32[]{:S(2)}) copy-start(s32[1,8,20]{2,1,0:T(8,128)} %param.9) | copy-start | bytes 1924
  4.1 19.1 %collective-permute-start.2 = (bf16[32,128,128]{2,1,0:T(8,128)(2,1)S(1)}, bf16[32,128,128]{2,1,0:T(8,128)(2,1)S(1)}, u32[]{:S(2)}, u32[]{:S(2)}) collective-permute-start(bf16[32,128,128]{2,1,0:T(8,128)(2,1)S(1)} %pad_maximum_fusion.refs_0_), channel_id=1, source_target_pairs={{10,2},{14,6},{0,8},{18,10},{4,12},{22,14},{8,16},{26,18},{12,20},... | collective-permute-start | bytes 3145736 | tf_op jit(solution)/shard_map/ppermute | solution.py:331
  7.7 0.7 %copy-start.5 = (s32[36]{0:T(128)S(1)}, s32[36]{0:T(128)}, u32[]{:S(2)}) copy-start(s32[36]{0:T(128)} %constant.47.clone) | copy-start | bytes 436
  8.9 0.7 %copy-start.3 = (s32[1,8]{1,0:T(1,128)S(1)}, s32[1,8]{1,0:T(1,128)}, u32[]{:S(2)}) copy-start(s32[1,8]{1,0:T(1,128)} %param.10) | copy-start | bytes 100
  12.1 8.6 %collective-permute-start.1 = (bf16[1040,128]{1,0:T(8,128)(2,1)S(1)}, bf16[1040,128]{1,0:T(8,128)(2,1)S(1)}, u32[]{:S(2)}, u32[]{:S(2)}) collective-permute-start(bf16[1040,128]{1,0:T(8,128)(2,1)S(1)} %pad_maximum_fusion.1), channel_id=1, source_target_pairs={{1,0},{0,1},{3,2},{2,3},{5,4},{4,5},{7,6},{6,7},{9,8},{8,9},{11,10... | collective-permute-start | bytes 798728 | tf_op jit(solution)/shard_map/ppermute | solution.py:331
  14.8 13.3 %collective-permute-start.3 = (bf16[7,128,128]{2,1,0:T(8,128)(2,1)S(1)}, bf16[7,128,128]{2,1,0:T(8,128)(2,1)S(1)}, u32[]{:S(2)}, u32[]{:S(2)}) collective-permute-start(bf16[7,128,128]{2,1,0:T(8,128)(2,1)S(1)} %slice.48), channel_id=1, source_target_pairs={{8,4},{10,6},{4,8},{6,10},{16,12},{18,14},{12,16},{14,18},{24,20},... | collective-permute-start | bytes 688136 | tf_op jit(solution)/shard_map/ppermute | solution.py:331
  16.8 12.1 %collective-permute-start.7 = (bf16[9,128,128]{2,1,0:T(8,128)(2,1)S(1)}, bf16[9,128,128]{2,1,0:T(8,128)(2,1)S(1)}, u32[]{:S(2)}, u32[]{:S(2)}) collective-permute-start(bf16[9,128,128]{2,1,0:T(8,128)(2,1)S(1)} %slice.50), channel_id=1, source_target_pairs={{12,4},{14,6},{0,8},{2,10},{20,12},{22,14},{8,16},{10,18},{28,20},... | collective-permute-start | bytes 884744 | tf_op jit(solution)/shard_map/ppermute | solution.py:331
  20.7 2.8 %collective-permute-start.5 = (bf16[16,128,128]{2,1,0:T(8,128)(2,1)S(1)}, bf16[16,128,128]{2,1,0:T(8,128)(2,1)S(1)}, u32[]{:S(2)}, u32[]{:S(2)}) collective-permute-start(bf16[16,128,128]{2,1,0:T(8,128)(2,1)S(1)} %collective-permute-done.4.refs_2_), channel_id=1, source_target_pairs={{2,0},{0,2},{6,4},{4,6},{10,8},{8,10},{14,12},{12,14},{18,16},{16,... | collective-permute-start | bytes 1572872 | tf_op jit(solution)/shard_map/ppermute | solution.py:331
  23.4 2.0 %collective-permute-start.6 = (bf16[16,128,128]{2,1,0:T(8,128)(2,1)S(1)}, bf16[16,128,128]{2,1,0:T(8,128)(2,1)S(1)}, u32[]{:S(2)}, u32[]{:S(2)}) collective-permute-start(bf16[16,128,128]{2,1,0:T(8,128)(2,1)S(1)} %slice.49), channel_id=1, source_target_pairs={{2,0},{0,2},{6,4},{4,6},{10,8},{8,10},{14,12},{12,14},{18,16},{16,... | collective-permute-start | bytes 1572872 | tf_op jit(solution)/shard_map/ppermute | solution.py:331
  28.1 1.9 %collective-permute-start.8 = (bf16[7,128,128]{2,1,0:T(8,128)(2,1)S(1)}, bf16[7,128,128]{2,1,0:T(8,128)(2,1)S(1)}, u32[]{:S(2)}, u32[]{:S(2)}) collective-permute-start(bf16[7,128,128]{2,1,0:T(8,128)(2,1)S(1)} %collective-permute-done.3.refs_4_), channel_id=1, source_target_pairs={{2,0},{0,2},{6,4},{4,6},{10,8},{8,10},{14,12},{12,14},{18,16},{16,... | collective-permute-start | bytes 688136 | tf_op jit(solution)/shard_map/ppermute | solution.py:331
  30.0 1.6 %collective-permute-start.9 = (bf16[9,128,128]{2,1,0:T(8,128)(2,1)S(1)}, bf16[9,128,128]{2,1,0:T(8,128)(2,1)S(1)}, u32[]{:S(2)}, u32[]{:S(2)}) collective-permute-start(bf16[9,128,128]{2,1,0:T(8,128)(2,1)S(1)} %collective-permute-done.7.refs_3_), channel_id=1, source_target_pairs={{2,0},{0,2},{6,4},{4,6},{10,8},{8,10},{14,12},{12,14},{18,16},{16,... | collective-permute-start | bytes 884744 | tf_op jit(solution)/shard_map/ppermute | solution.py:331
  33.3 9.2 %collective-permute-start.10 = (bf16[8,128,128]{2,1,0:T(8,128)(2,1)S(1)}, bf16[8,128,128]{2,1,0:T(8,128)(2,1)S(1)}, u32[]{:S(2)}, u32[]{:S(2)}) collective-permute-start(bf16[8,128,128]{2,1,0:T(8,128)(2,1)S(1)} %get-tuple-element.43), channel_id=1, source_target_pairs={{1,0},{0,1},{3,2},{2,3},{5,4},{4,5},{7,6},{6,7},{9,8},{8,9},{11,10... | collective-permute-start | bytes 786440 | tf_op jit(solution)/shard_map/ppermute | solution.py:331
  35.5 7.0 %collective-permute-start.11 = (f32[8,2,128]{2,1,0:T(2,128)S(1)}, f32[8,2,128]{2,1,0:T(2,128)S(1)}, u32[]{:S(2)}, u32[]{:S(2)}) collective-permute-start(f32[8,2,128]{2,1,0:T(2,128)S(1)} %get-tuple-element.44), channel_id=1, source_target_pairs={{1,0},{0,1},{3,2},{2,3},{5,4},{4,5},{7,6},{6,7},{9,8},{8,9},{11,10... | collective-permute-start | bytes 24584 | tf_op jit(solution)/shard_map/ppermute | solution.py:331
